TPU v7x, 256 devices: a whole 4x4x8 slice. The times are simulated.
256 devices in a mesh: noise: 8 (over z), row: 16 (over y, x), col: 2 (over core).
Axes of the slice: x: 4, y: 4, z: 8, core: 2. Of those that a mesh axis runs over, the one named last changes fastest.
Arguments:
- images: bfloat16 [256, 4, 6144], P('row', None, 'col'), may hold values from -40 to 40
- gain: float32 [6144], P('col'), may hold values from 0.3 to 3.5
- up_weight: bfloat16 [6144, 12288], P('col', 'row'), may hold values from -0.078125 to 0.078125
- down_weight: bfloat16 [12288, 6144], P('row', 'col'), may hold values from -0.0546875 to 0.0546875
- cotangent: bfloat16 [256, 16, 6144], P('row', 'noise', 'col'), may hold values from -6 to 6
- seeds: int32 [16], P('noise'), may hold values from 0 to 999999
- assign: int32 [16, 1], replicated, may hold values from 0 to 3, as said below
Outputs:
- saliency: float32 [256, 4, 6144], P('row', None, 'col')
Inputs may be any that keep to these rules, and one draw needn't show every extreme that they name: `assign`: every one of the 4 images is named by at least one copy.
All inputs are finite; a program needn't handle non-finite values.
Results may differ from a plain program's by a relative error of at most 0.0019.
Values may be sent and summed in bfloat16 or wider, within the bound.
A program may use at most 64 MiB of HBM per device.

v0:
```python
import math
import jax
import jax.numpy as jnp
from jax import lax
from jax.sharding import PartitionSpec as P

D = 6144
noise_scale = 0.6
gelu_coef = 0.044715
root_term = math.sqrt(2.0 / math.pi)


def mix_noise(seed_value, token_index, feature_index, width):
    linear = token_index[:, None] * width + feature_index[None, :]
    mixed = linear * 1664525 + seed_value * 1013904223
    mixed = mixed ^ mixed >> 13
    mixed = mixed * 1274126177
    mixed = mixed ^ mixed >> 16
    return ((mixed & 65535).astype(jnp.float32) - 32767.5) * (1.0 / 18918.0)


def gelu_slope(preact):
    inner = root_term * (preact + gelu_coef * preact * preact * preact)
    tanh_val = jnp.tanh(inner)
    return 0.5 * (1.0 + tanh_val) + 0.5 * preact * (1.0 - tanh_val * tanh_val) * root_term * (
        1.0 + 3.0 * gelu_coef * preact * preact
    )


def body(images, gain, up_weight, down_weight, cotangent, seeds, assign):
    slot_count = seeds.shape[0]
    tok_local = images.shape[0]
    image_count = images.shape[1]
    width_local = images.shape[2]
    col_index = lax.axis_index("col")
    row_index = lax.axis_index("row")
    noise_index = lax.axis_index("noise")
    image_ids = jnp.arange(image_count, dtype=jnp.int32)
    my_images = lax.dynamic_slice_in_dim(assign[:, 0], noise_index * slot_count, slot_count)
    onehot = (my_images[:, None] == image_ids[None, :]).astype(jnp.float32)
    clean_rows = jnp.einsum(
        "si,tid->tsd", onehot.astype(jnp.bfloat16), images, preferred_element_type=jnp.float32
    )
    token_index = row_index * tok_local + jnp.arange(tok_local, dtype=jnp.int32)
    feature_index = col_index * width_local + jnp.arange(width_local, dtype=jnp.int32)
    noise_field = jax.vmap(
        lambda seed_value: mix_noise(seed_value, token_index, feature_index, D), out_axes=1
    )(seeds)
    noisy_rows = clean_rows + noise_scale * noise_field
    feat_mean = lax.psum(jnp.sum(noisy_rows, axis=-1), "col") / D
    centred = noisy_rows - feat_mean[..., None]
    feat_var = lax.psum(jnp.sum(centred * centred, axis=-1), "col") / D
    inv_std = lax.rsqrt(feat_var + 1e-06)[..., None]
    normed = centred * inv_std
    scaled = (normed * gain).astype(jnp.bfloat16)
    gathered = (
        lax.all_gather(scaled, "row", axis=0, tiled=True),
        lax.all_gather(cotangent, "row", axis=0, tiled=True),
    )
    row_count = gathered[0].shape[0] * slot_count
    full_scaled = gathered[0].reshape(row_count, width_local)
    full_cotangent = gathered[1].reshape(row_count, width_local)
    preact_part = jnp.dot(full_scaled, up_weight, preferred_element_type=jnp.float32)
    back_part = jnp.einsum(
        "td,hd->th", full_cotangent, down_weight, preferred_element_type=jnp.float32
    )
    preact, back_grad = lax.psum((preact_part, back_part), "col")
    hidden_grad = (back_grad * gelu_slope(preact)).astype(jnp.bfloat16)
    scaled_grad = lax.psum_scatter(
        jnp.einsum("th,dh->td", hidden_grad, up_weight, preferred_element_type=jnp.float32),
        "row",
        scatter_dimension=0,
        tiled=True,
    )
    scaled_grad = scaled_grad.reshape(tok_local, slot_count, width_local)
    normed_grad = scaled_grad * gain
    grad_sum, grad_dot = lax.psum(
        (jnp.sum(normed_grad, axis=-1), jnp.sum(normed_grad * normed, axis=-1)), "col"
    )
    input_grad = cotangent.astype(jnp.float32) + inv_std * (
        normed_grad - grad_sum[..., None] / D - normed * (grad_dot[..., None] / D)
    )
    partial_totals = jnp.einsum("si,tsd->tid", onehot, input_grad, precision=lax.Precision.HIGHEST)
    onehot_all = (assign[:, 0][:, None] == image_ids[None, :]).astype(jnp.float32)
    counts = jnp.sum(onehot_all, axis=0)
    totals = lax.psum(partial_totals, "noise")
    return totals / counts[None, :, None]


def solution(mesh):
    placed = (
        P("row", None, "col"),
        P("col"),
        P("col", "row"),
        P("row", "col"),
        P("row", "noise", "col"),
        P("noise"),
        P(),
    )
    return jax.shard_map(
        body, mesh=mesh, in_specs=placed, out_specs=P("row", None, "col"), check_vma=False
    )
```

profile of v0, /device:TPU:2, one launch (start us, length us, event | category | flops | bytes accessed | tf_op | source)
XLA Modules:
  0.0 361.4 jit_solution(3402559265118721403)
XLA Ops:
  6.6 0.7 broadcast_multiply_fusion.3
  7.3 0.7 dynamic-slice_bitcast_fusion
  8.1 0.9 fusion.41
  9.0 2.5 psum.49
  11.5 0.4 multiply_reduce_fusion.2
  11.8 2.5 psum.50
  14.3 1.0 multiply_convert_fusion
  15.4 0.7 all-gather.3.cloned.1.call-update
  16.1 54.5 %all-gather.5.cloned.1.call-done = bf16[256,2,3072]{2,1,0:T(2,128)(2,1)} async-done(((bf16[16,2,3072]{2,1,0:T(2,128)(2,1)}), bf16[256,2,3072]{2,1,0:T(2,128)(2,1)}) %all-gather.5.cloned.1.call-update) | async-done | bytes 3145744 | tf_op jit(solution)/shard_map/all_gather | solution.py:57
  70.6 7.5 %reshape.60 = bf16[512,3072]{1,0:T(8,128)(2,1)} reshape(bf16[256,2,3072]{2,1,0:T(2,128)(2,1)} %all-gather.5.cloned.1.call-done) | data formatting | bytes 6291456 | tf_op jit(solution)/shard_map/reshape | solution.py:61
  78.2 7.1 %fusion.43 = f32[512,768]{1,0:T(8,128)} fusion(bf16[512,3072]{1,0:T(8,128)(2,1)} %reshape.60, bf16[3072,768]{1,0:T(8,128)(2,1)} %param.9), kind=kOutput, calls=%fused_computation.66 | convolution fusion | flops 2415919104 | bytes 9437184 | tf_op jit(solution)/shard_map/dot_general | solution.py:63
  85.2 39.8 %all-gather.3.cloned.1.call-done = bf16[256,2,3072]{2,1,0:T(2,128)(2,1)} async-done(((bf16[16,2,3072]{2,1,0:T(2,128)(2,1)}), bf16[256,2,3072]{2,1,0:T(2,128)(2,1)}) %all-gather.3.cloned.1.call-update) | async-done | bytes 3145744 | tf_op jit(solution)/shard_map/all_gather | solution.py:58
  125.0 7.5 %reshape.59 = bf16[512,3072]{1,0:T(8,128)(2,1)} reshape(bf16[256,2,3072]{2,1,0:T(2,128)(2,1)} %all-gather.3.cloned.1.call-done) | data formatting | bytes 6291456 | tf_op jit(solution)/shard_map/reshape | solution.py:62
  132.6 7.1 %fusion.42 = f32[512,768]{1,0:T(8,128)} fusion(bf16[512,3072]{1,0:T(8,128)(2,1)} %reshape.59, bf16[768,3072]{1,0:T(8,128)(2,1)} %param.10), kind=kOutput, calls=%fused_computation.65 | convolution fusion | flops 2415919104 | bytes 9437184 | tf_op jit(solution)/shard_map/td,hd->th/dot_general | solution.py:64
  139.7 33.9 %all-reduce.7.cloned.1.call-done = (f32[512,768]{1,0:T(8,128)}, f32[512,768]{1,0:T(8,128)}) async-done(((f32[512,768]{1,0:T(8,128)}, f32[512,768]{1,0:T(8,128)}), (f32[512,768]{1,0:T(8,128)}, f32[512,768]{1,0:T(8,128)})) %all-reduce.7.cloned.1.call-update) | async-done | bytes 3145744 | tf_op jit(solution)/shard_map/psum | solution.py:67
  173.6 9.2 %fusion.8 = f32[512,3072]{1,0:T(8,128)} fusion(bf16[3072,768]{1,0:T(8,128)(2,1)} %param.9, f32[512,768]{1,0:T(8,128)} %get-tuple-element.7, f32[512,768]{1,0:T(8,128)} %get-tuple-element.8), kind=kOutput, calls=%fused_computation.12 | convolution fusion | flops 2423390208 | bytes 14155776 | tf_op jit(solution)/shard_map/th,dh->td/dot_general | solution.py:70
  182.8 0.2 all-reduce.5.cloned.1.call-start
  183.1 87.3 %reduce-scatter.2.cloned.1.call-done = f32[32,3072]{1,0:T(8,128)} async-done(((f32[512,3072]{1,0:T(8,128)}), f32[32,3072]{1,0:T(8,128)}) %reduce-scatter.2.cloned.1.call-update) | async-done | bytes 393232 | tf_op jit(solution)/shard_map/reduce_scatter | solution.py:69
  270.3 1.3 reshape.61
  271.6 0.5 multiply_reduce_fusion
  272.3 3.3 all-reduce
  275.7 2.3 convolution_bitcast_fusion
  278.1 74.4 %all-reduce.5.cloned.1.call-done = f32[16,4,3072]{2,1,0:T(4,128)} async-done(((f32[16,4,3072]{2,1,0:T(4,128)}), f32[16,4,3072]{2,1,0:T(4,128)}) %all-reduce.5.cloned.1.call-update) | async-done | bytes 786448 | tf_op jit(solution)/shard_map/psum | solution.py:86
  352.6 2.3 broadcast_divide_fusion
  (27 shorter events, 0.7 us)
Async XLA Ops:
  6.5 1.5 copy-start
  6.5 64.1 %all-gather.5.cloned.1.call-start = ((), (), s32[]{:S(2)}) async-start(), calls=%async_computation.2 | async-start | bytes 3342336 | tf_op jit(solution)/shard_map/all_gather | solution.py:57
  8.1 6.2 %copy-start.3 = (f32[3072]{0:T(1024)S(1)}, f32[3072]{0:T(1024)}, u32[]{:S(2)}) copy-start(f32[3072]{0:T(1024)} %param.8) | copy-start | bytes 36868
  15.3 109.7 %all-gather.3.cloned.1.call-start = ((), (), s32[]{:S(2)}) async-start(), calls=%async_computation.1 | async-start | bytes 3342336 | tf_op jit(solution)/shard_map/all_gather | solution.py:58
  16.1 157.5 %all-reduce.7.cloned.1.call-start = ((), (), s32[]{:S(2)}) async-start(), calls=%async_computation.5 | async-start | bytes 6291456 | tf_op jit(solution)/shard_map/psum | solution.py:67
  139.7 130.7 %reduce-scatter.2.cloned.1.call-start = ((), (), s32[]{:S(2)}) async-start(), calls=%async_computation.3 | async-start | bytes 6684672 | tf_op jit(solution)/shard_map/reduce_scatter | solution.py:69
  182.8 92.8 %copy-start.2 = (bf16[16,2,3072]{2,1,0:T(2,128)(2,1)S(1)}, bf16[16,2,3072]{2,1,0:T(2,128)(2,1)}, u32[]{:S(2)}) copy-start(bf16[16,2,3072]{2,1,0:T(2,128)(2,1)} %param.11) | copy-start | bytes 589828
  182.8 169.7 %all-reduce.5.cloned.1.call-start = ((), (), s32[]{:S(2)}) async-start(), calls=%async_computation.4 | async-start | bytes 1572864 | tf_op jit(solution)/shard_map/psum | solution.py:86
  270.3 1.8 copy-start.1
  275.7 2.4 copy-start.4
Sparse Core Ops, SparseCore 0:
  15.4 55.1 all-gather.4
  73.1 51.9 all-gather.2
  139.8 33.7 all-reduce.6
  182.9 87.3 reduce-scatter.1
  278.1 74.3 all-reduce.4
where the time goes:
time: 362 us; the launch traced here: 361 us
  waiting for transfers between devices  291 us (80%)
  matrix products  26.6 us (7%)
  local copies, waits for them, and re-layouts  17.2 us (5%)
  between operations  13.2 us (4%)
  blocking collectives  8.21 us (2%)
  other arithmetic  5.16 us (1%)
    reduce_scatter x1, waiting for transfers between devices, body(): lax.psum_scatter(jnp.einsum('th,dh->td', hidden_grad, up_weight, preferre...  87.3 us
    psum x1, waiting for transfers between devices, body(): totals = lax.psum(partial_totals, 'noise')  74.4 us
    all_gather x1, waiting for transfers between devices, body(): lax.all_gather(scaled, 'row', axis=0, tiled=True)  54.5 us
    all_gather x1, waiting for transfers between devices, body(): lax.all_gather(cotangent, 'row', axis=0, tiled=True)  39.8 us
    psum x1, waiting for transfers between devices, body(): preact, back_grad = lax.psum((preact_part, back_part), 'col')  33.9 us
    dot_general x1, matrix products, body(): jnp.einsum('th,dh->td', hidden_grad, up_weight, preferred_element_type=jn...  9.19 us
    reshape x1, local copies, waits for them, and re-layouts, body(): full_scaled = gathered[0].reshape(row_count, width_local)  7.54 us
    reshape x1, local copies, waits for them, and re-layouts, body(): full_cotangent = gathered[1].reshape(row_count, width_local)  7.51 us
  transfers between devices with their start and end apart: 5, of which 5 were waited for; matrix products, arithmetic and copies ran while one was open for 4% of the time, Pallas kernels for 0%

commit v1 on v0

--- a/solution.py
+++ b/solution.py
@@ -3,6 +3,7 @@
 import jax.numpy as jnp
 from jax import lax
 from jax.sharding import PartitionSpec as P
+from jax.lax import all_to_all, axis_size
 
 D = 6144
 noise_scale = 0.6
@@ -53,10 +54,10 @@
     inv_std = lax.rsqrt(feat_var + 1e-06)[..., None]
     normed = centred * inv_std
     scaled = (normed * gain).astype(jnp.bfloat16)
-    gathered = (
-        lax.all_gather(scaled, "row", axis=0, tiled=True),
-        lax.all_gather(cotangent, "row", axis=0, tiled=True),
+    side_direct = lambda mine: jnp.concatenate(
+        all_to_all(jnp.stack([mine for _ in range(axis_size("row"))]), "row", 0, 0), axis=0
     )
+    gathered = (lax.all_gather(scaled, "row", axis=0, tiled=True), side_direct(cotangent))
     row_count = gathered[0].shape[0] * slot_count
     full_scaled = gathered[0].reshape(row_count, width_local)
     full_cotangent = gathered[1].reshape(row_count, width_local)

time: 362 us -> 324 us (0.90)
  waiting for transfers between devices: 291 us -> 208 us
  blocking collectives: 8.21 us -> 57.3 us
    all_to_all x0 -> x1, blocking collectives: none -> 49 us  [body(): all_to_all(jnp.stack([mine for _ in range(axis_size('row'))]), 'row', 0, 0)]
    all_gather x1, waiting for transfers between devices: 54.5 us -> 12.7 us  [body(): lax.all_gather(scaled, 'row', axis=0, tiled=True)]
    all_gather x1 -> x0, waiting for transfers between devices: 39.8 us -> none  [body(): lax.all_gather(cotangent, 'row', axis=0, tiled=True)]
    reshape x1 -> x0, local copies, waits for them, and re-layouts: 7.51 us -> none  [body(): full_cotangent = gathered[1].reshape(row_count, width_local)]
    another operation x0 -> x2, local copies, waits for them, and re-layouts: none -> 5.13 us  [the longest x1 2.71 us: body(): full_cotangent = gathered[1].reshape(row_count, width_local)]
  transfers between devices with their start and end apart: 5 -> 4, of which waited for: 5 -> 4; matrix products, arithmetic and copies ran while one was open for 4% -> 4% of each run, Pallas kernels for 0% -> 0%
where the time goes in v1:
time: 324 us
  waiting for transfers between devices  208 us (64%)
  blocking collectives  57.3 us (18%)
  matrix products  25.6 us (8%)
  local copies, waits for them, and re-layouts  13.6 us (4%)
  between operations  13.3 us (4%)
  other arithmetic  5.15 us (2%)
    reduce_scatter x1, waiting for transfers between devices, body(): lax.psum_scatter(jnp.einsum('th,dh->td', hidden_grad, up_weight, preferre...  87.4 us
    psum x1, waiting for transfers between devices, body(): totals = lax.psum(partial_totals, 'noise')  74.4 us
    all_to_all x1, blocking collectives, body(): all_to_all(jnp.stack([mine for _ in range(axis_size('row'))]), 'row', 0, 0)  49 us
    psum x1, waiting for transfers between devices, body(): preact, back_grad = lax.psum((preact_part, back_part), 'col')  33.7 us
    all_gather x1, waiting for transfers between devices, body(): lax.all_gather(scaled, 'row', axis=0, tiled=True)  12.7 us
    dot_general x1, matrix products, body(): jnp.einsum('th,dh->td', hidden_grad, up_weight, preferred_element_type=jn...  9.19 us
    dot_general x1, matrix products, body(): jnp.einsum('td,hd->th', full_cotangent, down_weight, preferred_element_ty...  7.08 us
  transfers between devices with their start and end apart: 4, of which 4 were waited for; matrix products, arithmetic and copies ran while one was open for 4% of the time, Pallas kernels for 0%

profile of v1, /device:TPU:2, one launch (start us, length us, event | category | flops | bytes accessed | tf_op | source)
XLA Modules:
  0.0 323.5 jit_solution(8634527289678298368)
XLA Ops:
  6.6 0.7 broadcast_multiply_fusion.3
  7.3 0.7 dynamic-slice_bitcast_fusion
  8.1 0.9 fusion.41
  9.0 2.5 psum.49
  11.5 0.4 multiply_reduce_fusion.2
  11.9 2.5 psum.50
  14.3 1.0 multiply_convert_fusion
  15.4 2.4 stack.2
  17.8 49.0 %all_to_all.5 = bf16[16,16,2,3072]{3,2,1,0:T(2,128)(2,1)S(1)} all-to-all(bf16[16,16,2,3072]{3,2,1,0:T(2,128)(2,1)S(1)} %stack.2), channel_id=1, replica_groups=mesh['noise'=8,'row'=16,'col'=2] {'row'}, dimensions={0} | all-to-all | bytes 6291456 | tf_op jit(solution)/shard_map/all_to_all | solution.py:58
  66.9 2.7 reshape_reshape.3
  69.6 7.1 %fusion.42 = f32[512,768]{1,0:T(8,128)} fusion(bf16[512,3072]{1,0:T(8,128)(2,1)} %reshape_reshape.3, bf16[768,3072]{1,0:T(8,128)(2,1)} %param.10), kind=kOutput, calls=%fused_computation.65 | convolution fusion | flops 2415919104 | bytes 9437184 | tf_op jit(solution)/shard_map/td,hd->th/dot_general | solution.py:65
  76.7 12.7 %all-gather.2.cloned.1.call-done = bf16[256,2,3072]{2,1,0:T(2,128)(2,1)} async-done(((bf16[16,2,3072]{2,1,0:T(2,128)(2,1)}), bf16[256,2,3072]{2,1,0:T(2,128)(2,1)}) %all-gather.2.cloned.1.call-update) | async-done | bytes 3145744 | tf_op jit(solution)/shard_map/all_gather | solution.py:60
  89.4 6.3 %reshape.58 = bf16[512,3072]{1,0:T(8,128)(2,1)S(1)} reshape(bf16[256,2,3072]{2,1,0:T(2,128)(2,1)} %all-gather.2.cloned.1.call-done) | data formatting | bytes 6291456 | tf_op jit(solution)/shard_map/reshape | solution.py:62
  95.7 6.1 %fusion.43 = f32[512,768]{1,0:T(8,128)} fusion(bf16[512,3072]{1,0:T(8,128)(2,1)S(1)} %reshape.58, bf16[3072,768]{1,0:T(8,128)(2,1)} %param.9), kind=kOutput, calls=%fused_computation.66 | convolution fusion | flops 2415919104 | bytes 9437184 | tf_op jit(solution)/shard_map/dot_general | solution.py:64
  101.8 0.2 reduce-scatter.2.cloned.1.call-start
  102.1 33.7 %all-reduce.7.cloned.1.call-done = (f32[512,768]{1,0:T(8,128)}, f32[512,768]{1,0:T(8,128)}) async-done(((f32[512,768]{1,0:T(8,128)}, f32[512,768]{1,0:T(8,128)}), (f32[512,768]{1,0:T(8,128)}, f32[512,768]{1,0:T(8,128)})) %all-reduce.7.cloned.1.call-update) | async-done | bytes 3145744 | tf_op jit(solution)/shard_map/psum | solution.py:68
  135.8 9.2 %fusion.8 = f32[512,3072]{1,0:T(8,128)} fusion(bf16[3072,768]{1,0:T(8,128)(2,1)} %param.9, f32[512,768]{1,0:T(8,128)} %get-tuple-element.7, f32[512,768]{1,0:T(8,128)} %get-tuple-element.8), kind=kOutput, calls=%fused_computation.12 | convolution fusion | flops 2423390208 | bytes 14155776 | tf_op jit(solution)/shard_map/th,dh->td/dot_general | solution.py:71
  145.1 87.4 %reduce-scatter.2.cloned.1.call-done = f32[32,3072]{1,0:T(8,128)} async-done(((f32[512,3072]{1,0:T(8,128)}), f32[32,3072]{1,0:T(8,128)}) %reduce-scatter.2.cloned.1.call-update) | async-done | bytes 393232 | tf_op jit(solution)/shard_map/reduce_scatter | solution.py:70
  232.5 1.3 reshape.59
  233.8 0.5 multiply_reduce_fusion
  234.5 3.3 %all-reduce = (f32[16,2]{1,0:T(8,128)S(1)}, f32[16,2]{1,0:T(8,128)S(1)}) all-reduce(f32[16,2]{1,0:T(8,128)S(1)} %multiply_reduce_fusion, f32[16,2]{1,0:T(8,128)S(1)} %reduce_sum.50), channel_id=1, replica_groups=mesh['noise'=8,'row'=16,'col'=2] {'col'}, use_global_device_ids=true, to_apply=%region_10.0 | all-reduce | flops 64 | bytes 512 | tf_op jit(solution)/shard_map/psum | solution.py:78
  237.9 2.3 convolution_bitcast_fusion
  240.3 74.4 %all-reduce.5.cloned.1.call-done = f32[16,4,3072]{2,1,0:T(4,128)} async-done(((f32[16,4,3072]{2,1,0:T(4,128)}), f32[16,4,3072]{2,1,0:T(4,128)}) %all-reduce.5.cloned.1.call-update) | async-done | bytes 786448 | tf_op jit(solution)/shard_map/psum | solution.py:87
  314.7 2.3 broadcast_divide_fusion
  (38 shorter events, 0.7 us)
Async XLA Ops:
  6.5 1.5 copy-start
  6.5 82.9 %all-gather.2.cloned.1.call-start = ((), (), s32[]{:S(2)}) async-start(), calls=%async_computation.2 | async-start | bytes 3342336 | tf_op jit(solution)/shard_map/all_gather | solution.py:60
  8.0 1.0 copy-start.9
  8.1 6.3 %copy-start.6 = (f32[3072]{0:T(1024)S(1)}, f32[3072]{0:T(1024)}, u32[]{:S(2)}) copy-start(f32[3072]{0:T(1024)} %param.8) | copy-start | bytes 36868
  8.1 7.3 %copy-start.4 = (bf16[16,2,3072]{2,1,0:T(2,128)(2,1)S(1)}, bf16[16,2,3072]{2,1,0:T(2,128)(2,1)}, u32[]{:S(2)}) copy-start(bf16[16,2,3072]{2,1,0:T(2,128)(2,1)} %param.11) | copy-start | bytes 589828
  9.0 6.4 %copy-start.1 = (f32[16,2,3072]{2,1,0:T(2,128)}, f32[16,2,3072]{2,1,0:T(2,128)S(1)}, u32[]{:S(2)}) copy-start(f32[16,2,3072]{2,1,0:T(2,128)S(1)} %get-tuple-element.10) | copy-start | bytes 1179652
  15.3 120.4 %all-reduce.7.cloned.1.call-start = ((), (), s32[]{:S(2)}) async-start(), calls=%async_computation.5 | async-start | bytes 6291456 | tf_op jit(solution)/shard_map/psum | solution.py:68
  101.8 130.7 %reduce-scatter.2.cloned.1.call-start = ((), (), s32[]{:S(2)}) async-start(), calls=%async_computation.3 | async-start | bytes 6684672 | tf_op jit(solution)/shard_map/reduce_scatter | solution.py:70
  145.0 88.8 %copy-start.2 = (f32[16,2,3072]{2,1,0:T(2,128)S(1)}, f32[16,2,3072]{2,1,0:T(2,128)}, u32[]{:S(2)}) copy-start(f32[16,2,3072]{2,1,0:T(2,128)} %copy-done.1) | copy-start | bytes 1179652
  145.0 88.9 %copy-start.7 = (f32[3072]{0:T(1024)S(1)}, f32[3072]{0:T(1024)}, u32[]{:S(2)}) copy-start(f32[3072]{0:T(1024)} %param.8) | copy-start | bytes 36868
  145.0 92.8 %copy-start.5 = (bf16[16,2,3072]{2,1,0:T(2,128)(2,1)S(1)}, bf16[16,2,3072]{2,1,0:T(2,128)(2,1)}, u32[]{:S(2)}) copy-start(bf16[16,2,3072]{2,1,0:T(2,128)(2,1)} %param.11) | copy-start | bytes 589828
  145.0 92.8 %copy-start.10 = (s32[2]{0:T(128)S(1)}, s32[2]{0:T(128)}, u32[]{:S(2)}) copy-start(s32[2]{0:T(128)} %copy-done.9) | copy-start | bytes 28
  145.0 169.7 %all-reduce.5.cloned.1.call-start = ((), (), s32[]{:S(2)}) async-start(), calls=%async_computation.4 | async-start | bytes 1572864 | tf_op jit(solution)/shard_map/psum | solution.py:87
  232.5 1.8 copy-start.3
  237.9 2.4 copy-start.8
Sparse Core Ops, SparseCore 0:
  15.5 73.8 all-gather.1
  102.0 33.7 all-reduce.6
  145.1 87.3 reduce-scatter.1
  240.3 74.3 all-reduce.4
